TPU v7x, 256 devices: a whole 4x4x8 slice. The times are simulated.
256 devices in a mesh: ctx: 32 (over x_hi, z, core), head: 8 (over x_lo, y).
Axes of the slice: x: 4 (x_hi: 2, x_lo: 2; x = x_hi * 2 + x_lo), y: 4, z: 8, core: 2. Of those that a mesh axis runs over, the one named last changes fastest.
Arguments:
- queries_one: bfloat16 [4096, 4096], P('ctx', 'head'), may hold values from -6 to 6
- grads_one: bfloat16 [4096, 4096], P('ctx', 'head'), may hold values from -6 to 6
- queries_two: bfloat16 [4096, 4096], P('ctx', 'head'), may hold values from -6 to 6
- grads_two: bfloat16 [4096, 4096], P('ctx', 'head'), may hold values from -6 to 6
- key_rows: bfloat16 [4096, 1024], P('ctx', 'head'), may hold values from -6 to 6
- value_rows: bfloat16 [4096, 1024], P('ctx', 'head'), may hold values from -6 to 6
- shared_input: bfloat16 [4096, 8192], P('ctx'), may hold values from -6 to 6
- key_weight: bfloat16 [8192, 1024], P(None, 'head'), may hold values from -0.09375 to 0.09375
- value_weight: bfloat16 [8192, 1024], P(None, 'head'), may hold values from -0.0625 to 0.0625
- block_order: int32 [64], replicated, may hold values from 0 to 63, as said below
Outputs:
- query_grad_one: bfloat16 [4096, 4096], P('ctx', 'head')
- query_grad_two: bfloat16 [4096, 4096], P('ctx', 'head')
- input_grad: bfloat16 [4096, 8192], P('ctx', 'head')
- key_weight_grad: float32 [8192, 1024], P('ctx', 'head')
- value_weight_grad: float32 [8192, 1024], P('ctx', 'head')
Inputs may be any that keep to these rules, and one draw needn't show every extreme that they name: `block_order`: each block 0 to 63 once; slots 2c and 2c + 1 hold blocks i and 63 - i for some i.
All inputs are finite; a program needn't handle non-finite values.
Results may differ from a plain program's by a relative error of at most 0.013.
Values may be sent and summed in bfloat16 or wider, within the bound.
No kernel may reach another device: no remote copies, remote signals or barrier semaphores. Data moves between devices by JAX's collectives and lax.ppermute only.
A program may use at most 128 MiB of HBM per device.

v0:
```python
import math
import jax
import jax.numpy as jnp
from jax import lax
from jax.sharding import PartitionSpec as P

H = 32
KV = 8
DH = 128


def attend(queries, grads, query_pos, keys_pos, values_pos, key_pos, scale):
    scores = (
        jnp.einsum("rkgd,jkd->kgrj", queries, keys_pos, preferred_element_type=jnp.float32) * scale
    )
    allowed = key_pos[None, :] <= query_pos[:, None]
    scores = jnp.where(allowed, scores, -jnp.inf)
    peak = jnp.max(scores, axis=-1, keepdims=True)
    weights = jnp.exp(scores - peak)
    probabilities = weights / jnp.sum(weights, axis=-1, keepdims=True)
    prob_low = probabilities.astype(jnp.bfloat16)
    dprob = jnp.einsum("rkgd,jkd->kgrj", grads, values_pos, preferred_element_type=jnp.float32)
    row_delta = jnp.sum(probabilities * dprob, axis=-1, keepdims=True)
    dscore = (probabilities * (dprob - row_delta) * scale).astype(jnp.bfloat16)
    dquery = jnp.einsum(
        "kgrj,jkd->rkgd", dscore, keys_pos, preferred_element_type=jnp.float32
    ).astype(jnp.bfloat16)
    dkey = jnp.einsum("kgrj,rkgd->jkd", dscore, queries, preferred_element_type=jnp.float32)
    dvalue = jnp.einsum("kgrj,rkgd->jkd", prob_low, grads, preferred_element_type=jnp.float32)
    return (dquery, dkey, dvalue)


def on_device(
    queries_one,
    grads_one,
    queries_two,
    grads_two,
    key_rows,
    value_rows,
    shared_input,
    key_weight,
    value_weight,
    block_order,
):
    rows_local = queries_one.shape[0]
    half_rows = rows_local // 2
    ctx_count = lax.axis_size("ctx")
    seq_len = rows_local * ctx_count
    kv_local = key_rows.shape[1] // DH
    group = H // KV
    scale = 1.0 / math.sqrt(DH)
    gathered_keys, gathered_values = (
        lax.all_gather(key_rows, "ctx", axis=0, tiled=True),
        lax.all_gather(value_rows, "ctx", axis=0, tiled=True),
    )
    inverse = jnp.argsort(block_order)

    def to_position(slotted):
        return slotted.reshape(2 * ctx_count, half_rows, kv_local * DH)[inverse].reshape(
            seq_len, kv_local, DH
        )

    def to_slot(positioned):
        return positioned.reshape(2 * ctx_count, half_rows, kv_local * DH)[block_order].reshape(
            seq_len, kv_local * DH
        )

    keys_pos = to_position(gathered_keys)
    values_pos = to_position(gathered_values)
    key_pos = jnp.arange(seq_len, dtype=jnp.int32)
    own_blocks = lax.dynamic_slice_in_dim(block_order, 2 * lax.axis_index("ctx"), 2)
    query_pos = (
        own_blocks[:, None] * half_rows + jnp.arange(half_rows, dtype=jnp.int32)[None, :]
    ).reshape(rows_local)

    def layer_grads(queries, grads):
        query_four = queries.reshape(rows_local, kv_local, group, DH)
        grad_four = grads.reshape(rows_local, kv_local, group, DH)
        dquery, dkey, dvalue = attend(
            query_four, grad_four, query_pos, keys_pos, values_pos, key_pos, scale
        )
        return (dquery.reshape(rows_local, kv_local * group * DH), to_slot(dkey), to_slot(dvalue))

    dq_one, dk_one, dv_one = layer_grads(queries_one, grads_one)
    dq_two, dk_two, dv_two = layer_grads(queries_two, grads_two)
    key_total, value_total = (
        lax.psum_scatter(dk_one + dk_two, "ctx", scatter_dimension=0, tiled=True),
        lax.psum_scatter(dv_one + dv_two, "ctx", scatter_dimension=0, tiled=True),
    )
    key_grad = key_total.astype(jnp.bfloat16)
    value_grad = value_total.astype(jnp.bfloat16)
    contract_cols = (((1,), (1,)), ((), ()))
    input_term = lax.dot_general(
        key_grad, key_weight, contract_cols, preferred_element_type=jnp.float32
    )
    input_term = input_term + lax.dot_general(
        value_grad, value_weight, contract_cols, preferred_element_type=jnp.float32
    )
    input_grad = lax.psum_scatter(input_term, "head", scatter_dimension=1, tiled=True).astype(
        jnp.bfloat16
    )
    both_grads = jnp.concatenate([key_grad, value_grad], axis=1)
    width = key_grad.shape[1]
    contract_rows = (((0,), (0,)), ((), ()))
    weight_grad = lax.psum_scatter(
        lax.dot_general(
            shared_input, both_grads, contract_rows, preferred_element_type=jnp.float32
        ),
        "ctx",
        scatter_dimension=0,
        tiled=True,
    )
    return (dq_one, dq_two, input_grad, weight_grad[:, :width], weight_grad[:, width:])


def solution(mesh):
    return jax.shard_map(
        on_device,
        mesh=mesh,
        in_specs=(
            P("ctx", "head"),
            P("ctx", "head"),
            P("ctx", "head"),
            P("ctx", "head"),
            P("ctx", "head"),
            P("ctx", "head"),
            P("ctx", None),
            P(None, "head"),
            P(None, "head"),
            P(),
        ),
        out_specs=(
            P("ctx", "head"),
            P("ctx", "head"),
            P("ctx", "head"),
            P("ctx", "head"),
            P("ctx", "head"),
        ),
        check_vma=False,
    )
```

profile of v0, /device:TPU:8, one launch (start us, length us, event | category | flops | bytes accessed | tf_op | source)
XLA Modules:
  0.0 679.7 jit_solution(15424929762015373111)
XLA Ops:
  9.6 2.7 sort.17
  14.1 77.1 %all-gather.5.cloned.1.call-done = bf16[4096,128]{1,0:T(8,128)(2,1)} async-done(((bf16[128,128]{1,0:T(8,128)(2,1)}), bf16[4096,128]{1,0:T(8,128)(2,1)}) %all-gather.5.cloned.1.call-update) | async-done | bytes 1048592 | tf_op jit(solution)/shard_map/all_gather | solution.py:54
  91.2 2.9 gather_fusion.1
  94.1 74.3 %all-gather.3.cloned.1.call-done = bf16[4096,128]{1,0:T(8,128)(2,1)} async-done(((bf16[128,128]{1,0:T(8,128)(2,1)}), bf16[4096,128]{1,0:T(8,128)(2,1)}) %all-gather.3.cloned.1.call-update) | async-done | bytes 1048592 | tf_op jit(solution)/shard_map/all_gather | solution.py:53
  168.5 2.0 gather_fusion
  170.4 2.4 fusion.48
  172.9 1.3 fusion.47
  175.3 5.1 fusion.4
  180.4 5.5 fusion.12
  185.9 2.7 fusion.29
  189.7 4.3 fusion
  194.0 4.7 fusion.13
  198.8 1.9 copy-done.2
  200.7 2.6 fusion.23
  203.3 3.6 gather_fusion.2
  206.9 3.6 gather_fusion.3
  210.5 4.1 add.63
  215.0 6.2 fusion.14
  221.2 3.6 gather_fusion.5
  224.8 6.4 fusion.16
  231.1 3.6 gather_fusion.4
  234.7 4.1 add.65
  239.0 92.0 %reduce-scatter.5.cloned.1.call-done = f32[128,128]{1,0:T(8,128)} async-done(((f32[4096,128]{1,0:T(8,128)}), f32[128,128]{1,0:T(8,128)}) %reduce-scatter.5.cloned.1.call-update) | async-done | bytes 65552 | tf_op jit(solution)/shard_map/reduce_scatter | solution.py:87
  331.8 4.3 fusion.49
  336.1 116.7 %reduce-scatter.7.cloned.1.call-done = f32[128,128]{1,0:T(8,128)} async-done(((f32[4096,128]{1,0:T(8,128)}), f32[128,128]{1,0:T(8,128)}) %reduce-scatter.7.cloned.1.call-update) | async-done | bytes 65552 | tf_op jit(solution)/shard_map/reduce_scatter | solution.py:88
  453.6 5.5 convolution_add_fusion
  459.2 4.5 convolution_bitcast_fusion
  463.7 2.9 convolution_convert_fusion.1
  467.5 3.3 convolution_convert_fusion
  471.5 39.2 %reduce-scatter.9.cloned.1.call-done = f32[128,1024]{1,0:T(8,128)} async-done(((f32[128,8192]{1,0:T(8,128)}), f32[128,1024]{1,0:T(8,128)}) %reduce-scatter.9.cloned.1.call-update) | async-done | bytes 524304 | tf_op jit(solution)/shard_map/reduce_scatter | solution.py:99
  510.7 1.8 convert_element_type.51
  512.5 157.9 %reduce-scatter.11.cloned.1.call-done = f32[256,256]{0,1:T(8,128)} async-done(((f32[8192,256]{0,1:T(8,128)}), f32[256,256]{0,1:T(8,128)}) %reduce-scatter.11.cloned.1.call-update) | async-done | bytes 262160 | tf_op jit(solution)/shard_map/reduce_scatter | solution.py:105
  (51 shorter events, 12.6 us)
Async XLA Ops:
  7.2 452.0 %copy-start = (bf16[128,8192]{1,0:T(8,128)(2,1)S(1)}, bf16[128,8192]{1,0:T(8,128)(2,1)}, u32[]{:S(2)}) copy-start(bf16[128,8192]{1,0:T(8,128)(2,1)} %param.16) | copy-start | bytes 6291460
  7.2 165.7 %copy-start.7 = (bf16[128,512]{1,0:T(8,128)(2,1)S(1)}, bf16[128,512]{1,0:T(8,128)(2,1)}, u32[]{:S(2)}) copy-start(bf16[128,512]{1,0:T(8,128)(2,1)} %param.10) | copy-start | bytes 393220
  7.2 84.0 %all-gather.5.cloned.1.call-start = ((), (), s32[]{:S(2)}) async-start(), calls=%async_computation.5 | async-start | bytes 1081344 | tf_op jit(solution)/shard_map/all_gather | solution.py:54
  7.9 160.5 %all-gather.3.cloned.1.call-start = ((), (), s32[]{:S(2)}) async-start(), calls=%async_computation.4 | async-start | bytes 1081344 | tf_op jit(solution)/shard_map/all_gather | solution.py:53
  8.7 322.3 %reduce-scatter.5.cloned.1.call-start = ((), (), s32[]{:S(2)}) async-start(), calls=%async_computation.6 | async-start | bytes 2162688 | tf_op jit(solution)/shard_map/reduce_scatter | solution.py:87
  170.4 2.5 copy-start.6
  172.9 21.1 %copy-start.4 = (f32[1,4,128,4096]{2,3,1,0:T(8,128)}, f32[1,4,128,4096]{2,3,1,0:T(8,128)S(1)}, u32[]{:S(2)}) copy-start(f32[1,4,128,4096]{2,3,1,0:T(8,128)S(1)} %get-tuple-element.24) | copy-start | bytes 25165828
  172.9 2.4 copy-start.5
  172.9 2.4 copy-start.10
  174.2 6.2 copy-start.3
  185.9 8.1 %copy-start.1 = (bf16[4,128,4096]{1,2,0:T(8,128)(2,1)}, bf16[4,128,4096]{1,2,0:T(8,128)(2,1)S(1)}, u32[]{:S(2)}) copy-start(bf16[4,128,4096]{1,2,0:T(8,128)(2,1)S(1)} %fusion.12) | copy-start | bytes 12582916
  185.9 3.8 copy-start.9
  194.0 6.7 copy-start.8
  198.8 1.9 copy-start.2
  214.7 238.1 %reduce-scatter.7.cloned.1.call-start = ((), (), s32[]{:S(2)}) async-start(), calls=%async_computation.7 | async-start | bytes 2162688 | tf_op jit(solution)/shard_map/reduce_scatter | solution.py:88
  238.9 271.8 %reduce-scatter.9.cloned.1.call-start = ((), (), s32[]{:S(2)}) async-start(), calls=%async_computation.8 | async-start | bytes 4718592 | tf_op jit(solution)/shard_map/reduce_scatter | solution.py:99
  459.2 211.2 %reduce-scatter.11.cloned.1.call-start = ((), (), s32[]{:S(2)}) async-start(), calls=%async_computation.9 | async-start | bytes 8650752 | tf_op jit(solution)/shard_map/reduce_scatter | solution.py:105
Sparse Core Ops, SparseCore 0:
  10.8 80.3 all-gather.4
  94.0 74.4 all-gather.2
  214.8 116.1 reduce-scatter.4
  335.6 117.1 reduce-scatter.6
  459.3 51.4 reduce-scatter.8
  515.0 155.3 reduce-scatter.10
where the time goes:
time: 680 us
  waiting for transfers between devices  559 us (82%)
  matrix products  51.4 us (8%)
  other arithmetic  29.5 us (4%)
  local copies, waits for them, and re-layouts  25.4 us (4%)
  between operations  14.3 us (2%)
    reduce_scatter x1, waiting for transfers between devices, on_device(): lax.psum_scatter(lax.dot_general(shared_input, both_grads, contract_rows,...  158 us
    reduce_scatter x1, waiting for transfers between devices, on_device(): lax.psum_scatter(dv_one + dv_two, 'ctx', scatter_dimension=0, tiled=True)  117 us
    reduce_scatter x1, waiting for transfers between devices, on_device(): lax.psum_scatter(dk_one + dk_two, 'ctx', scatter_dimension=0, tiled=True)  92 us
    all_gather x1, waiting for transfers between devices, on_device(): lax.all_gather(value_rows, 'ctx', axis=0, tiled=True)  77.1 us
    all_gather x1, waiting for transfers between devices, on_device(): lax.all_gather(key_rows, 'ctx', axis=0, tiled=True)  74.3 us
    reduce_scatter x1, waiting for transfers between devices, on_device(): lax.psum_scatter(input_term, 'head', scatter_dimension=1, tiled=True)  39.2 us
    gather x4, local copies, waits for them, and re-layouts, to_slot(): positioned.reshape(2 * ctx_count, half_rows, kv_local * DH)[block_order]  14.5 us
  transfers between devices with their start and end apart: 6, of which 6 were waited for; matrix products, arithmetic and copies ran while one was open for 8% of the time, Pallas kernels for 0%

commit v1 on v0

--- a/solution.py
+++ b/solution.py
@@ -51,7 +51,9 @@
     scale = 1.0 / math.sqrt(DH)
     gathered_keys, gathered_values = (
         lax.all_gather(key_rows, "ctx", axis=0, tiled=True),
-        lax.all_gather(value_rows, "ctx", axis=0, tiled=True),
+        jnp.concatenate(
+            lax.all_to_all(jnp.stack([value_rows] * lax.axis_size("ctx")), "ctx", 0, 0), axis=0
+        ),
     )
     inverse = jnp.argsort(block_order)
 

time: 680 us -> 609 us (0.90)
  waiting for transfers between devices: 559 us -> 474 us
  starting transfers between devices: 0.46 us -> 11.9 us
    all_gather x1 -> x0, waiting for transfers between devices: 77.1 us -> none  [on_device(): lax.all_gather(value_rows, 'ctx', axis=0, tiled=True)]
    all_to_all x0 -> x1, starting transfers between devices: none -> 11.4 us  [on_device(): lax.all_to_all(jnp.stack([value_rows] * lax.axis_size('ctx')), 'ctx', 0, 0)]
    all_gather x1, waiting for transfers between devices: 74.3 us -> 67.1 us  [on_device(): lax.all_gather(key_rows, 'ctx', axis=0, tiled=True)]
  transfers between devices with their start and end apart: 6 -> 6, of which waited for: 6 -> 5; matrix products, arithmetic and copies ran while one was open for 8% -> 9% of each run, Pallas kernels for 0% -> 0%
where the time goes in v1:
time: 609 us; the launch traced here: 608 us
  waiting for transfers between devices  474 us (78%)
  matrix products  51.4 us (8%)
  other arithmetic  29.5 us (5%)
  local copies, waits for them, and re-layouts  27.4 us (4%)
  between operations  14 us (2%)
  starting transfers between devices  11.9 us (2%)
    reduce_scatter x1, waiting for transfers between devices, on_device(): lax.psum_scatter(lax.dot_general(shared_input, both_grads, contract_rows,...  158 us
    reduce_scatter x1, waiting for transfers between devices, on_device(): lax.psum_scatter(dv_one + dv_two, 'ctx', scatter_dimension=0, tiled=True)  117 us
    reduce_scatter x1, waiting for transfers between devices, on_device(): lax.psum_scatter(dk_one + dk_two, 'ctx', scatter_dimension=0, tiled=True)  92.1 us
    all_gather x1, waiting for transfers between devices, on_device(): lax.all_gather(key_rows, 'ctx', axis=0, tiled=True)  67.1 us
    reduce_scatter x1, waiting for transfers between devices, on_device(): lax.psum_scatter(input_term, 'head', scatter_dimension=1, tiled=True)  39.2 us
    gather x4, local copies, waits for them, and re-layouts, to_slot(): positioned.reshape(2 * ctx_count, half_rows, kv_local * DH)[block_order]  14.4 us
    dot_general x2, matrix products, attend(): jnp.einsum('kgrj,rkgd->jkd', prob_low, grads, preferred_element_type=jnp....  12.6 us
  transfers between devices with their start and end apart: 6, of which 5 were waited for; matrix products, arithmetic and copies ran while one was open for 9% of the time, Pallas kernels for 0%

profile of v1, /device:TPU:8, one launch (start us, length us, event | category | flops | bytes accessed | tf_op | source)
XLA Modules:
  0.0 607.8 jit_solution(16527270083623148641)
XLA Ops:
  7.9 2.0 stack.2
  9.9 11.4 %all-to-all-start = ((bf16[32,128,128]{2,1,0:T(8,128)(2,1)}), bf16[32,128,128]{2,1,0:T(8,128)(2,1)}, u32[]{:S(2)}, u32[]{:S(2)}) async-start(bf16[32,128,128]{2,1,0:T(8,128)(2,1)} %stack.2), calls=%async_computation | async-start | bytes 2097152 | tf_op jit(solution)/shard_map/all_to_all | solution.py:55
  22.3 2.7 sort.17
  26.8 67.1 %all-gather.2.cloned.1.call-done = bf16[4096,128]{1,0:T(8,128)(2,1)} async-done(((bf16[128,128]{1,0:T(8,128)(2,1)}), bf16[4096,128]{1,0:T(8,128)(2,1)}) %all-gather.2.cloned.1.call-update) | async-done | bytes 1048592 | tf_op jit(solution)/shard_map/all_gather | solution.py:53
  93.9 2.0 gather_fusion
  95.8 2.9 gather_fusion.1
  98.8 2.4 fusion.48
  103.6 5.1 fusion.4
  108.7 5.5 fusion.12
  114.2 2.7 fusion.29
  118.1 4.3 fusion
  122.3 4.7 fusion.13
  127.1 1.9 copy-done.2
  129.0 2.6 fusion.23
  131.6 3.6 gather_fusion.2
  135.2 3.6 gather_fusion.3
  138.8 4.1 add.63
  143.3 6.2 %fusion.14 = f32[4096,128,1]{1,0,2:T(8,128)} fusion(f32[1,4,128,4096]{2,3,1,0:T(8,128)} %copy-done.4, f32[4,128]{1,0:T(4,128)S(1)} %fusion.11, f32[4,128]{1,0:T(4,128)S(1)} %get-tuple-element.23, bf16[128,512]{1,0:T(8,128)(2,1)S(1)} %copy-done.9), kind=kOutput, calls=%fused_computation.30 | convolution fusion | flops 543162368 | bytes 10620928 | tf_op jit(solution)/shard_map/kgrj,rkgd->jkd/dot_general | solution.py:29
  149.5 3.6 gather_fusion.5
  153.1 6.4 %fusion.16 = f32[4096,128,1]{1,0,2:T(8,128)} fusion(f32[1,4,128,4096]{2,3,1,0:T(8,128)} %copy-done.3, f32[4,128]{1,0:T(4,128)S(1)} %fusion.9, f32[4,128]{1,0:T(4,128)S(1)} %get-tuple-element.19, bf16[128,512]{1,0:T(8,128)(2,1)S(1)} %copy-done.10), kind=kOutput, calls=%fused_computation.32 | convolution fusion | flops 543162368 | bytes 10620928 | tf_op jit(solution)/shard_map/kgrj,rkgd->jkd/dot_general | solution.py:29
  159.4 3.6 gather_fusion.4
  163.0 4.1 add.65
  167.3 92.1 %reduce-scatter.5.cloned.1.call-done = f32[128,128]{1,0:T(8,128)} async-done(((f32[4096,128]{1,0:T(8,128)}), f32[128,128]{1,0:T(8,128)}) %reduce-scatter.5.cloned.1.call-update) | async-done | bytes 65552 | tf_op jit(solution)/shard_map/reduce_scatter | solution.py:89
  260.2 4.3 fusion.49
  264.5 116.9 %reduce-scatter.7.cloned.1.call-done = f32[128,128]{1,0:T(8,128)} async-done(((f32[4096,128]{1,0:T(8,128)}), f32[128,128]{1,0:T(8,128)}) %reduce-scatter.7.cloned.1.call-update) | async-done | bytes 65552 | tf_op jit(solution)/shard_map/reduce_scatter | solution.py:90
  382.2 5.5 convolution_add_fusion
  387.8 4.5 convolution_bitcast_fusion
  392.3 2.9 convolution_convert_fusion.1
  396.0 3.3 convolution_convert_fusion
  400.1 39.2 %reduce-scatter.9.cloned.1.call-done = f32[128,1024]{1,0:T(8,128)} async-done(((f32[128,8192]{1,0:T(8,128)}), f32[128,1024]{1,0:T(8,128)}) %reduce-scatter.9.cloned.1.call-update) | async-done | bytes 524304 | tf_op jit(solution)/shard_map/reduce_scatter | solution.py:101
  439.3 1.8 convert_element_type.51
  441.1 157.6 %reduce-scatter.11.cloned.1.call-done = f32[256,256]{0,1:T(8,128)} async-done(((f32[8192,256]{0,1:T(8,128)}), f32[256,256]{0,1:T(8,128)}) %reduce-scatter.11.cloned.1.call-update) | async-done | bytes 262160 | tf_op jit(solution)/shard_map/reduce_scatter | solution.py:107
  (51 shorter events, 13.2 us)
Async XLA Ops:
  7.2 380.6 %copy-start = (bf16[128,8192]{1,0:T(8,128)(2,1)S(1)}, bf16[128,8192]{1,0:T(8,128)(2,1)}, u32[]{:S(2)}) copy-start(bf16[128,8192]{1,0:T(8,128)(2,1)} %param.16) | copy-start | bytes 6291460
  7.2 86.7 %all-gather.2.cloned.1.call-start = ((), (), s32[]{:S(2)}) async-start(), calls=%async_computation.5 | async-start | bytes 1081344 | tf_op jit(solution)/shard_map/all_gather | solution.py:53
  9.9 85.9 %all-to-all-start = ((bf16[32,128,128]{2,1,0:T(8,128)(2,1)}), bf16[32,128,128]{2,1,0:T(8,128)(2,1)}, u32[]{:S(2)}, u32[]{:S(2)}) async-start(bf16[32,128,128]{2,1,0:T(8,128)(2,1)} %stack.2), calls=%async_computation | async-start | bytes 2097152 | tf_op jit(solution)/shard_map/all_to_all | solution.py:55
  21.3 79.8 %copy-start.7 = (bf16[128,512]{1,0:T(8,128)(2,1)S(1)}, bf16[128,512]{1,0:T(8,128)(2,1)}, u32[]{:S(2)}) copy-start(bf16[128,512]{1,0:T(8,128)(2,1)} %param.10) | copy-start | bytes 393220
  21.4 238.0 %reduce-scatter.5.cloned.1.call-start = ((), (), s32[]{:S(2)}) async-start(), calls=%async_computation.6 | async-start | bytes 2162688 | tf_op jit(solution)/shard_map/reduce_scatter | solution.py:89
  98.7 2.4 copy-start.6
  101.2 21.1 %copy-start.4 = (f32[1,4,128,4096]{2,3,1,0:T(8,128)}, f32[1,4,128,4096]{2,3,1,0:T(8,128)S(1)}, u32[]{:S(2)}) copy-start(f32[1,4,128,4096]{2,3,1,0:T(8,128)S(1)} %get-tuple-element.24) | copy-start | bytes 25165828
  101.2 2.4 copy-start.5
  101.2 2.4 copy-start.10
  102.5 6.2 %copy-start.3 = (f32[1,4,128,4096]{2,3,1,0:T(8,128)}, f32[1,4,128,4096]{2,3,1,0:T(8,128)S(1)}, u32[]{:S(2)}) copy-start(f32[1,4,128,4096]{2,3,1,0:T(8,128)S(1)} %get-tuple-element.20) | copy-start | bytes 25165828
  114.2 8.1 %copy-start.1 = (bf16[4,128,4096]{1,2,0:T(8,128)(2,1)}, bf16[4,128,4096]{1,2,0:T(8,128)(2,1)S(1)}, u32[]{:S(2)}) copy-start(bf16[4,128,4096]{1,2,0:T(8,128)(2,1)S(1)} %fusion.12) | copy-start | bytes 12582916
  114.2 3.8 copy-start.9
  122.3 6.7 %copy-start.8 = (bf16[128,512]{1,0:T(8,128)(2,1)S(1)}, bf16[128,512]{1,0:T(8,128)(2,1)}, u32[]{:S(2)}) copy-start(bf16[128,512]{1,0:T(8,128)(2,1)} %param.12) | copy-start | bytes 393220
  127.1 1.9 copy-start.2
  143.0 238.4 %reduce-scatter.7.cloned.1.call-start = ((), (), s32[]{:S(2)}) async-start(), calls=%async_computation.7 | async-start | bytes 2162688 | tf_op jit(solution)/shard_map/reduce_scatter | solution.py:90
  167.2 272.1 %reduce-scatter.9.cloned.1.call-start = ((), (), s32[]{:S(2)}) async-start(), calls=%async_computation.8 | async-start | bytes 4718592 | tf_op jit(solution)/shard_map/reduce_scatter | solution.py:101
  387.7 211.0 %reduce-scatter.11.cloned.1.call-start = ((), (), s32[]{:S(2)}) async-start(), calls=%async_computation.9 | async-start | bytes 8650752 | tf_op jit(solution)/shard_map/reduce_scatter | solution.py:107
Sparse Core Ops, SparseCore 0:
  10.8 83.0 all-gather.1
  143.1 116.2 reduce-scatter.4
  264.1 117.2 reduce-scatter.6
  387.8 51.4 reduce-scatter.8
  443.6 155.1 reduce-scatter.10
